TPU v7x, 32 devices: a whole 2x2x4 slice. The times are simulated.
32 devices in a mesh: dp: 4 (over y, x), expert: 8 (over z, core).
Axes of the slice: x: 2, y: 2, z: 4, core: 2. Of those that a mesh axis runs over, the one named last changes fastest.
Arguments:
- tokens: bfloat16 [4096, 2048], P(('dp', 'expert')), may hold values from -6 to 6
- expert_ids: int32 [4096, 3], P(('dp', 'expert')), may hold values from 0 to 7, all different within a row; in each aligned block of 128 rows (0 to 127, 128 to 255, ...) at most 64 rows name the same one
- gate_level: int32 [4096, 3], P(('dp', 'expert')), may hold values from 0 to 15
- cost_bucket: int32 [64], P(('dp', 'expert')), may hold values from 0 to 7
- gate_table: float32 [8, 16], replicated, may hold values from 0.05 to 0.6
- gate_weight: bfloat16 [8, 2048, 768], P('expert', 'dp'), may hold values from -0.125 to 0.125
- up_weight: bfloat16 [8, 2048, 768], P('expert', 'dp'), may hold values from -0.125 to 0.125
- down_weight: bfloat16 [8, 2048, 768], P('expert', 'dp'), may hold values from -0.21875 to 0.21875
- out_grad: bfloat16 [4096, 2048], P(('dp', 'expert')), may hold values from -6 to 6
Outputs:
- output: bfloat16 [4096, 2048], P(('dp', 'expert'))
- token_grad: bfloat16 [4096, 2048], P(('dp', 'expert'))
- gate_grad: float32 [8, 2048, 768], P('expert', 'dp')
- up_grad: float32 [8, 2048, 768], P('expert', 'dp')
- down_grad: float32 [8, 2048, 768], P('expert', 'dp')
Inputs may be any that keep to these rules, and one draw needn't show every extreme that they name: `expert_ids`: each row names 3 different experts. Among the rows of one device (aligned blocks of 128 rows) no expert is named more than 64 times, and in every draw some expert is named exactly 64 times in some block.
All inputs are finite; a program needn't handle non-finite values.
Results may differ from a plain program's by a relative error of at most 0.0085.
Values may be sent and summed in bfloat16 or wider, within the bound.
A program may use at most 128 MiB of HBM per device.

v0:
```python
import jax
import jax.numpy as jnp
from jax import lax
from jax.sharding import PartitionSpec as P


def move_rows(buffer):
    return lax.all_to_all(buffer, "expert", split_axis=0, concat_axis=0, tiled=True)


def shards(
    tokens,
    expert_ids,
    gate_level,
    cost_bucket,
    gate_table,
    gate_weight,
    up_weight,
    down_weight,
    out_grad,
):
    local_tokens = tokens.shape[0]
    top_count = expert_ids.shape[1]
    model_width = tokens.shape[1]
    members = lax.axis_size("expert")
    capacity = min(local_tokens, 4 * local_tokens * top_count // (3 * members))
    slot_total = members * capacity
    pair_total = local_tokens * top_count
    contract_last = (((1,), (1,)), ((), ()))
    contract_first = (((0,), (0,)), ((), ()))
    gathered = (
        lax.all_gather(gate_weight, "dp", axis=1, tiled=True),
        lax.all_gather(up_weight, "dp", axis=1, tiled=True),
        lax.all_gather(down_weight, "dp", axis=1, tiled=True),
    )
    w_gate = gathered[0][0]
    w_up = gathered[1][0]
    w_down = gathered[2][0]
    flat_ids = expert_ids.reshape(-1)
    marks_hot = (flat_ids[:, None] == jnp.arange(members, dtype=jnp.int32)[None, :]).astype(
        jnp.int32
    )
    earlier = jnp.cumsum(marks_hot, axis=0) - marks_hot
    slot_index = jnp.sum(earlier * marks_hot, axis=1)
    slot_place = flat_ids * capacity + slot_index
    owner_row = (
        jnp.full((slot_total,), pair_total, jnp.int32)
        .at[slot_place]
        .set(jnp.arange(pair_total, dtype=jnp.int32))
    )
    filled = owner_row < pair_total
    source_token = jnp.where(filled, owner_row // top_count, local_tokens)
    bucket_tok = jnp.repeat(cost_bucket, local_tokens // cost_bucket.shape[0])
    bucket_hot = (
        bucket_tok[:, None] == jnp.arange(gate_table.shape[0], dtype=jnp.int32)[None, :]
    ).astype(jnp.float32)
    table_rows = jnp.dot(bucket_hot, gate_table, precision=lax.Precision.HIGHEST)
    level_hot = (
        gate_level[:, :, None] == jnp.arange(gate_table.shape[1], dtype=jnp.int32)[None, None, :]
    ).astype(jnp.float32)
    gate_values = jnp.sum(level_hot * table_rows[:, None, :], axis=2)
    gate_padded = jnp.concatenate([gate_values.reshape(-1), jnp.zeros((1,), jnp.float32)])
    slot_gate = gate_padded[owner_row]
    zero_row = jnp.zeros((1, model_width), jnp.bfloat16)
    tokens_padded = jnp.concatenate([tokens, zero_row], axis=0)
    send_rows = tokens_padded[source_token].reshape(members, capacity, model_width)
    expert_rows = move_rows(send_rows).reshape(slot_total, model_width)
    gate_act = jnp.dot(expert_rows, w_gate, preferred_element_type=jnp.float32)
    up_act = jnp.dot(expert_rows, w_up, preferred_element_type=jnp.float32)
    sigmoid_gate = jax.nn.sigmoid(gate_act)
    swish_gate = gate_act * sigmoid_gate
    hidden = (swish_gate * up_act).astype(jnp.bfloat16)
    result = lax.dot_general(
        hidden, w_down, contract_last, preferred_element_type=jnp.float32
    ).astype(jnp.bfloat16)
    returned_rows = move_rows(result.reshape(members, capacity, model_width)).reshape(
        slot_total, model_width
    )
    picked = (
        returned_rows[slot_place].reshape(local_tokens, top_count, model_width).astype(jnp.float32)
    )
    output = jnp.sum(picked * gate_values[:, :, None], axis=1).astype(jnp.bfloat16)
    grad_padded = jnp.concatenate([out_grad, zero_row], axis=0)
    scaled = (grad_padded[source_token].astype(jnp.float32) * slot_gate[:, None]).astype(
        jnp.bfloat16
    )
    grad_rows = move_rows(scaled.reshape(members, capacity, model_width)).reshape(
        slot_total, model_width
    )
    grad_hidden = jnp.dot(grad_rows, w_down, preferred_element_type=jnp.float32)
    grad_gate_act = (
        grad_hidden * up_act * sigmoid_gate * (1.0 + gate_act * (1.0 - sigmoid_gate))
    ).astype(jnp.bfloat16)
    grad_up_act = (grad_hidden * swish_gate).astype(jnp.bfloat16)
    grad_in = (
        lax.dot_general(grad_gate_act, w_gate, contract_last, preferred_element_type=jnp.float32)
        + lax.dot_general(grad_up_act, w_up, contract_last, preferred_element_type=jnp.float32)
    ).astype(jnp.bfloat16)
    grad_back = move_rows(grad_in.reshape(members, capacity, model_width)).reshape(
        slot_total, model_width
    )
    token_grad = jnp.sum(
        grad_back[slot_place].reshape(local_tokens, top_count, model_width).astype(jnp.float32),
        axis=1,
    ).astype(jnp.bfloat16)
    both_act = jnp.concatenate([grad_gate_act, grad_up_act], axis=1)
    hidden_units = w_gate.shape[1]
    first_part = lax.dot_general(
        expert_rows, both_act, contract_first, preferred_element_type=jnp.float32
    )
    second_part = lax.dot_general(
        grad_rows, hidden, contract_first, preferred_element_type=jnp.float32
    )
    weight_sums = lax.psum_scatter(
        jnp.concatenate([first_part, second_part], axis=1).astype(jnp.bfloat16),
        "dp",
        scatter_dimension=0,
        tiled=True,
    ).astype(jnp.float32)
    gate_grad = weight_sums[:, :hidden_units][None]
    up_grad = weight_sums[:, hidden_units : 2 * hidden_units][None]
    down_grad = weight_sums[:, 2 * hidden_units :][None]
    return (output, token_grad, gate_grad, up_grad, down_grad)


def solution(mesh):
    return jax.shard_map(
        shards,
        mesh=mesh,
        in_specs=(
            P(("dp", "expert"), None),
            P(("dp", "expert"), None),
            P(("dp", "expert"), None),
            P(("dp", "expert")),
            P(),
            P("expert", "dp", None),
            P("expert", "dp", None),
            P("expert", "dp", None),
            P(("dp", "expert"), None),
        ),
        out_specs=(
            P(("dp", "expert"), None),
            P(("dp", "expert"), None),
            P("expert", "dp", None),
            P("expert", "dp", None),
            P("expert", "dp", None),
        ),
        check_vma=False,
    )
```

profile of v0, /device:TPU:11, one launch (start us, length us, event | category | flops | bytes accessed | tf_op | source)
XLA Modules:
  0.0 320.2 jit_solution(6029644549299537514)
XLA Ops:
  7.2 0.7 all-gather.8.cloned.1.call-update
  8.0 0.7 all-gather.6.cloned.1.call-update
  8.7 0.7 broadcast_multiply_fusion
  9.4 0.8 copy.28
  10.2 0.2 eq.57
  10.4 0.9 reduce-window.6
  11.2 0.2 slice_reduce_fusion
  11.5 0.2 eq.53
  11.8 0.2 mul.69
  12.0 0.7 broadcast_in_dim.18
  13.0 0.8 select_reduce_fusion
  13.9 0.2 reshape.105
  14.3 2.9 scatter_custom_fusion
  17.2 3.5 %gather_fusion.3 = f32[512]{0:T(512)S(1)} fusion(f32[385]{0:T(512)S(1)} %pad_maximum_fusion.1, s32[1024]{0:T(1024)S(1)} %get-tuple-element.28), kind=kCustom, calls=%fused_computation.3 | custom fusion | bytes 6144 | tf_op jit(solution)/shard_map/gather | solution.py:63
  20.9 2.5 gather_fusion.2
  23.3 1.7 fusion
  25.1 5.8 %all-to-all-start.2 = ((bf16[8,64,2048]{2,1,0:T(8,128)(2,1)}), bf16[8,64,2048]{2,1,0:T(8,128)(2,1)S(1)}, u32[]{:S(2)}, u32[]{:S(2)}) async-start(bf16[8,64,2048]{2,1,0:T(8,128)(2,1)} %fusion), calls=%async_computation.2 | async-start | bytes 4194304 | tf_op jit(solution)/shard_map/all_to_all | solution.py:8
  30.9 0.7 all-gather.4.cloned.1.call-update
  31.7 3.3 %gather_fusion = bf16[512,2048]{1,0:T(8,128)(2,1)} fusion(bf16[129,2048]{1,0:T(8,128)(2,1)S(1)} %concatenate.16, s32[1024]{0:T(1024)S(1)} %get-tuple-element.29), kind=kCustom, calls=%fused_computation | custom fusion | bytes 4196352 | tf_op jit(solution)/shard_map/gather | solution.py:66
  34.9 41.4 %all-to-all-done.2 = bf16[8,64,2048]{2,1,0:T(8,128)(2,1)S(1)} async-done(((bf16[8,64,2048]{2,1,0:T(8,128)(2,1)}), bf16[8,64,2048]{2,1,0:T(8,128)(2,1)S(1)}, u32[]{:S(2)}, u32[]{:S(2)}) %all-to-all-start.2) | async-done | bytes 2097184 | tf_op jit(solution)/shard_map/all_to_all | solution.py:8
  76.4 7.8 %all-to-all-start = ((bf16[8,64,2048]{2,1,0:T(8,128)(2,1)}), bf16[8,64,2048]{2,1,0:T(8,128)(2,1)}, u32[]{:S(2)}, u32[]{:S(2)}) async-start(bf16[8,64,2048]{2,1,0:T(8,128)(2,1)} %bitcast.2), calls=%async_computation | async-start | bytes 4194304 | tf_op jit(solution)/shard_map/all_to_all | solution.py:8
  84.2 4.8 %fusion.1 = f32[512,768]{1,0:T(8,128)} fusion(bf16[512,2048]{1,0:T(8,128)(2,1)S(1)} %bitcast.57, bf16[1,2048,768]{2,1,0:T(8,128)(2,1)} %all-gather.8.cloned.1.call-done), kind=kOutput, calls=%fused_computation.13 | convolution fusion | flops 1610612736 | bytes 6815744 | tf_op jit(solution)/shard_map/dot_general | solution.py:90
  89.0 40.7 %all-to-all-done = bf16[8,64,2048]{2,1,0:T(8,128)(2,1)} async-done(((bf16[8,64,2048]{2,1,0:T(8,128)(2,1)}), bf16[8,64,2048]{2,1,0:T(8,128)(2,1)}, u32[]{:S(2)}, u32[]{:S(2)}) %all-to-all-start) | async-done | bytes 2097184 | tf_op jit(solution)/shard_map/all_to_all | solution.py:8
  129.7 5.4 %fusion.7 = f32[512,768]{1,0:T(8,128)} fusion(bf16[512,2048]{1,0:T(8,128)(2,1)} %bitcast.3, bf16[1,2048,768]{2,1,0:T(8,128)(2,1)} %all-gather.6.cloned.1.call-done), kind=kOutput, calls=%fused_computation.19 | convolution fusion | flops 1610612736 | bytes 6815744 | tf_op jit(solution)/shard_map/dot_general | solution.py:69
  135.1 11.6 %all-gather.4.cloned.1.call-done = bf16[1,2048,768]{2,1,0:T(8,128)(2,1)} async-done(((bf16[1,512,768]{2,1,0:T(8,128)(2,1)}), bf16[1,2048,768]{2,1,0:T(8,128)(2,1)}) %all-gather.4.cloned.1.call-update) | async-done | bytes 3145744 | tf_op jit(solution)/shard_map/all_gather | solution.py:32
  146.7 5.8 %multiply_convert_fusion.1 = (bf16[512,768]{1,0:T(8,128)(2,1)S(1)}, bf16[512,768]{1,0:T(8,128)(2,1)S(1)}, bf16[512,768]{1,0:T(8,128)(2,1)S(1)}) fusion(f32[512,768]{1,0:T(8,128)} %fusion.1, f32[512,768]{1,0:T(8,128)} %fusion.7, bf16[512,2048]{1,0:T(8,128)(2,1)} %bitcast.3, bf16[1,2048,768]{2,1,0:T(8,128)(2,1)} %all-gather.4.cloned.1.call-done), kind=kOutput, calls=%fused_computation.33 | convolution fusion | flops 1616510976 | bytes 10747904 | tf_op jit(solution)/shard_map/dot_general | solution.py:68
  152.5 1.9 convolution_convert_fusion.1
  154.4 5.4 %convolution_convert_fusion = bf16[2048,1536]{0,1:T(8,128)(2,1)S(1)} fusion(bf16[512,2048]{1,0:T(8,128)(2,1)} %bitcast.3, bf16[512,768]{1,0:T(8,128)(2,1)S(1)} %get-tuple-element.24, bf16[512,768]{1,0:T(8,128)(2,1)S(1)} %get-tuple-element.23), kind=kOutput, calls=%fused_computation.7 | convolution fusion | flops 3227516928 | bytes 9961472 | tf_op jit(solution)/shard_map/dot_general | solution.py:108
  159.8 11.5 %pad_maximum_fusion = bf16[2048,2304]{0,1:T(8,128)(2,1)} fusion(bf16[2048,768]{0,1:T(8,128)(2,1)S(1)} %convolution_convert_fusion.1, bf16[2048,1536]{0,1:T(8,128)(2,1)S(1)} %convolution_convert_fusion), kind=kLoop, calls=%fused_computation.6 | loop fusion | flops 18874368 | bytes 18874368 | tf_op jit(solution)/shard_map/concatenate | solution.py:115
  171.4 1.1 copy-done.9
  172.5 5.1 %fusion.13 = bf16[512,2048]{1,0:T(8,128)(2,1)} fusion(bf16[512,768]{1,0:T(8,128)(2,1)S(1)} %copy-done.9, bf16[1,2048,768]{2,1,0:T(8,128)(2,1)} %all-gather.8.cloned.1.call-done), kind=kOutput, calls=%fused_computation.25 | convolution fusion | flops 1611661312 | bytes 6029312 | tf_op jit(solution)/shard_map/dot_general | solution.py:73
  177.6 5.4 %all-to-all-start.1 = ((bf16[8,64,2048]{2,1,0:T(8,128)(2,1)}), bf16[8,64,2048]{2,1,0:T(8,128)(2,1)S(1)}, u32[]{:S(2)}, u32[]{:S(2)}) async-start(bf16[8,64,2048]{2,1,0:T(8,128)(2,1)} %bitcast.60), calls=%async_computation.1 | async-start | bytes 4194304 | tf_op jit(solution)/shard_map/all_to_all | solution.py:8
  183.1 4.4 %fusion.5 = f32[512,2048]{1,0:T(8,128)S(1)} fusion(bf16[512,768]{1,0:T(8,128)(2,1)} %copy-done.7, bf16[1,2048,768]{2,1,0:T(8,128)(2,1)} %all-gather.6.cloned.1.call-done), kind=kOutput, calls=%fused_computation.17 | convolution fusion | flops 1610612736 | bytes 8126464 | tf_op jit(solution)/shard_map/dot_general | solution.py:97
  187.5 3.1 add_convert_fusion
  190.6 38.0 %all-to-all-done.1 = bf16[8,64,2048]{2,1,0:T(8,128)(2,1)S(1)} async-done(((bf16[8,64,2048]{2,1,0:T(8,128)(2,1)}), bf16[8,64,2048]{2,1,0:T(8,128)(2,1)S(1)}, u32[]{:S(2)}, u32[]{:S(2)}) %all-to-all-start.1) | async-done | bytes 2097184 | tf_op jit(solution)/shard_map/all_to_all | solution.py:8
  228.6 7.8 %all-to-all-start.3 = ((bf16[8,64,2048]{2,1,0:T(8,128)(2,1)}), bf16[8,64,2048]{2,1,0:T(8,128)(2,1)}, u32[]{:S(2)}, u32[]{:S(2)}) async-start(bf16[8,64,2048]{2,1,0:T(8,128)(2,1)} %bitcast.59), calls=%async_computation.3 | async-start | bytes 4194304 | tf_op jit(solution)/shard_map/all_to_all | solution.py:8
  236.4 3.1 gather_fusion.1
  239.5 5.5 %reshape.110 = f32[128,3,2048]{2,1,0:T(4,128)} reshape(bf16[384,2048]{1,0:T(8,128)(2,1)} %gather_fusion.1) | data formatting | bytes 4718592 | tf_op jit(solution)/shard_map/convert_element_type | solution.py:80
  245.0 36.9 %all-to-all-done.3 = bf16[8,64,2048]{2,1,0:T(8,128)(2,1)} async-done(((bf16[8,64,2048]{2,1,0:T(8,128)(2,1)}), bf16[8,64,2048]{2,1,0:T(8,128)(2,1)}, u32[]{:S(2)}, u32[]{:S(2)}) %all-to-all-start.3) | async-done | bytes 2097184 | tf_op jit(solution)/shard_map/all_to_all | solution.py:8
  281.9 6.9 %gather_fusion.4 = bf16[384,2048]{1,0:T(8,128)(2,1)} fusion(bf16[512,2048]{1,0:T(8,128)(2,1)} %bitcast.12, s32[1024]{0:T(1024)S(1)} %pad_clamp_fusion.1), kind=kCustom, calls=%fused_computation.4 | custom fusion | bytes 3147264 | tf_op jit(solution)/shard_map/gather | solution.py:103
  288.8 4.3 %reshape.109 = bf16[128,3,2048]{2,1,0:T(4,128)(2,1)S(1)} reshape(bf16[384,2048]{1,0:T(8,128)(2,1)} %gather_fusion.4) | data formatting | bytes 3145728 | tf_op jit(solution)/shard_map/reshape | solution.py:103
  293.1 4.0 %reduce_sum.45 = bf16[128,2048]{1,0:T(8,128)(2,1)} reduce(bf16[128,3,2048]{2,1,0:T(4,128)(2,1)S(1)} %reshape.109, bf16[]{:T(256)} %constant.14.clone.1), dimensions={1}, to_apply=%region_6.7 | reduce | flops 524288 | bytes 2097154 | tf_op jit(solution)/shard_map/reduce_sum | solution.py:102
  297.0 6.2 %multiply_reduce_fusion = bf16[128,2048]{1,0:T(8,128)(2,1)} fusion(f32[128,3,2048]{2,1,0:T(4,128)} %reshape.110, f32[128,3]{1,0:T(8,128)S(1)} %copy.30), kind=kLoop, calls=%fused_computation.11 | loop fusion | flops 1310720 | bytes 3671552 | tf_op jit(solution)/shard_map/reduce_sum | solution.py:82
  303.2 2.3 convert_element_type.63
  305.6 1.8 slice_bitcast_fusion
  307.4 3.0 copy.32
  310.4 1.6 copy.33
  312.0 1.6 copy.34
  (43 shorter events, 1.0 us)
Async XLA Ops:
  7.2 5.7 %copy-start = (f32[8,16]{1,0:T(8,128)S(1)}, f32[8,16]{1,0:T(8,128)}, u32[]{:S(2)}) copy-start(f32[8,16]{1,0:T(8,128)} %param.13) | copy-start | bytes 1540
  7.2 13.6 %copy-start.2 = (bf16[128,2048]{1,0:T(8,128)(2,1)S(1)}, bf16[128,2048]{1,0:T(8,128)(2,1)}, u32[]{:S(2)}) copy-start(bf16[128,2048]{1,0:T(8,128)(2,1)} %param.17) | copy-start | bytes 1572868
  7.2 77.0 %all-gather.8.cloned.1.call-start = ((), (), s32[]{:S(2)}) async-start(), calls=%async_computation.7 | async-start | bytes 3932160 | tf_op jit(solution)/shard_map/all_gather | solution.py:34
  7.9 121.7 %all-gather.6.cloned.1.call-start = ((), (), s32[]{:S(2)}) async-start(), calls=%async_computation.6 | async-start | bytes 3932160 | tf_op jit(solution)/shard_map/all_gather | solution.py:33
  25.1 6.5 %copy-start.3 = (bf16[128,2048]{1,0:T(8,128)(2,1)S(1)}, bf16[128,2048]{1,0:T(8,128)(2,1)}, u32[]{:S(2)}) copy-start(bf16[128,2048]{1,0:T(8,128)(2,1)} %param.9) | copy-start | bytes 1572868
  25.1 51.3 %all-to-all-start.2 = ((bf16[8,64,2048]{2,1,0:T(8,128)(2,1)}), bf16[8,64,2048]{2,1,0:T(8,128)(2,1)S(1)}, u32[]{:S(2)}, u32[]{:S(2)}) async-start(bf16[8,64,2048]{2,1,0:T(8,128)(2,1)} %fusion), calls=%async_computation.2 | async-start | bytes 4194304 | tf_op jit(solution)/shard_map/all_to_all | solution.py:8
  30.9 115.9 %all-gather.4.cloned.1.call-start = ((), (), s32[]{:S(2)}) async-start(), calls=%async_computation.5 | async-start | bytes 3932160 | tf_op jit(solution)/shard_map/all_gather | solution.py:32
  76.4 53.3 %all-to-all-start = ((bf16[8,64,2048]{2,1,0:T(8,128)(2,1)}), bf16[8,64,2048]{2,1,0:T(8,128)(2,1)}, u32[]{:S(2)}, u32[]{:S(2)}) async-start(bf16[8,64,2048]{2,1,0:T(8,128)(2,1)} %bitcast.2), calls=%async_computation | async-start | bytes 4194304 | tf_op jit(solution)/shard_map/all_to_all | solution.py:8
  84.2 219.1 %reduce-scatter.2.cloned.1.call-start = ((), (), s32[]{:S(2)}) async-start(), calls=%async_computation.8 | async-start | bytes 11796480 | tf_op jit(solution)/shard_map/reduce_scatter | solution.py:114
  152.5 1.9 copy-start.8
  152.5 1.9 copy-start.5
  152.5 1.9 copy-start.7
  171.4 1.1 copy-start.9
  177.6 51.0 %all-to-all-start.1 = ((bf16[8,64,2048]{2,1,0:T(8,128)(2,1)}), bf16[8,64,2048]{2,1,0:T(8,128)(2,1)S(1)}, u32[]{:S(2)}, u32[]{:S(2)}) async-start(bf16[8,64,2048]{2,1,0:T(8,128)(2,1)} %bitcast.60), calls=%async_computation.1 | async-start | bytes 4194304 | tf_op jit(solution)/shard_map/all_to_all | solution.py:8
  183.1 4.4 %copy-start.4 = (bf16[1,2048,768]{2,1,0:T(8,128)(2,1)S(1)}, bf16[1,2048,768]{2,1,0:T(8,128)(2,1)}, u32[]{:S(2)}) copy-start(bf16[1,2048,768]{2,1,0:T(8,128)(2,1)} %all-gather.4.cloned.1.call-done) | copy-start | bytes 9437188
  183.1 4.4 %copy-start.6 = (bf16[512,768]{1,0:T(8,128)(2,1)S(1)}, bf16[512,768]{1,0:T(8,128)(2,1)}, u32[]{:S(2)}) copy-start(bf16[512,768]{1,0:T(8,128)(2,1)} %copy-done.5) | copy-start | bytes 2359300
  228.6 53.3 %all-to-all-start.3 = ((bf16[8,64,2048]{2,1,0:T(8,128)(2,1)}), bf16[8,64,2048]{2,1,0:T(8,128)(2,1)}, u32[]{:S(2)}, u32[]{:S(2)}) async-start(bf16[8,64,2048]{2,1,0:T(8,128)(2,1)} %bitcast.59), calls=%async_computation.3 | async-start | bytes 4194304 | tf_op jit(solution)/shard_map/all_to_all | solution.py:8
  310.4 3.2 %copy-start.1 = (f32[8,16]{1,0:T(8,128)S(1)}, f32[8,16]{1,0:T(8,128)}, u32[]{:S(2)}) copy-start(f32[8,16]{1,0:T(8,128)} %param.13) | copy-start | bytes 1540
Sparse Core Ops, SparseCore 0:
  9.9 45.1 all-gather.7
  56.9 43.9 all-gather.5
  102.7 43.9 all-gather.3
  171.5 94.8 reduce-scatter.1
where the time goes:
time: 326 us; the launch traced here: 320 us
  waiting for transfers between devices  171 us (52%)
  local copies, waits for them, and re-layouts  44.2 us (14%)
  matrix products  36.1 us (11%)
  other arithmetic  28.3 us (9%)
  starting transfers between devices  26.9 us (8%)
  between operations  14 us (4%)
    all_to_all x4, waiting for transfers between devices, move_rows(): lax.all_to_all(buffer, 'expert', split_axis=0, concat_axis=0, tiled=True)  157 us
    all_to_all x4, starting transfers between devices, move_rows(): lax.all_to_all(buffer, 'expert', split_axis=0, concat_axis=0, tiled=True)  26.8 us
    all_gather x1, waiting for transfers between devices, shards(): lax.all_gather(gate_weight, 'dp', axis=1, tiled=True)  11.6 us
    concatenate x1, other arithmetic, shards(): jnp.concatenate([first_part, second_part], axis=1).astype(jnp.bfloat16)  11.5 us
    unnamed x24, local copies, waits for them, and re-layouts  8.19 us
    gather x1, local copies, waits for them, and re-layouts, shards(): grad_back[slot_place].reshape(local_tokens, top_count, model_width)  6.91 us
  transfers between devices with their start and end apart: 8, of which 5 were waited for; matrix products, arithmetic and copies ran while one was open for 23% of the time, Pallas kernels for 0%

commit v1 on v0

--- a/solution.py
+++ b/solution.py
@@ -1,7 +1,403 @@
+import functools
+
 import jax
 import jax.numpy as jnp
 from jax import lax
+from jax.experimental import pallas as pl
+from jax.experimental.pallas import tpu as pltpu
 from jax.sharding import PartitionSpec as P
+
+MESH = pl.DeviceIdType.MESH
+
+
+def places():
+    d = lax.axis_index("dp")
+    e = lax.axis_index("expert")
+    x = lax.rem(d, 2)
+    y = lax.div(d, 2)
+    return d, e, y * 2 + (1 - x), (1 - y) * 2 + x, (1 - y) * 2 + (1 - x)
+
+
+def gather_kernel(
+    chips,
+    wg, wu, wd, tok, grd, meta,
+    og, ou, od, otok, ogrd, ometa,
+    wsend, wrecv, zsend, zrecv, csend, crecv, local,
+):
+    d, e, dx, dy, _ = places()
+    z = lax.div(e, 2)
+    core = lax.rem(e, 2)
+    sibling = z * 2 + 1 - core
+    rows = wg.shape[1]
+    half = rows // 2
+    here_x, here_y = (dx, e), (dy, e)
+
+    barrier = pltpu.get_barrier_semaphore()
+    pl.semaphore_signal(barrier, inc=1, device_id=here_x, device_id_type=MESH)
+    pl.semaphore_signal(barrier, inc=1, device_id=here_y, device_id_type=MESH)
+    for k in range(1, 2 * chips):
+        pl.semaphore_signal(
+            barrier, inc=1, device_id=(d, lax.rem(e + k, 2 * chips)), device_id_type=MESH
+        )
+    pl.semaphore_wait(barrier, 2 * chips + 1)
+
+    weights = ((wg, og), (wu, ou), (wd, od))
+    blocks = ((tok, otok), (grd, ogrd), (meta, ometa))
+
+    def own_half(w, h):
+        return weights[w][0].at[0, pl.ds(h * half, half), :]
+
+    def placed(w, owner, h):
+        return weights[w][1].at[pl.ds(pl.multiple_of(owner * rows + h * half, half), half), :]
+
+    def wcopy(w, kind, src, dst, device):
+        return pltpu.make_async_remote_copy(
+            src_ref=src, dst_ref=dst, send_sem=wsend.at[w, kind], recv_sem=wrecv.at[w, kind],
+            device_id=device, device_id_type=MESH,
+        )
+
+    def wcopies(w):
+        return (
+            wcopy(w, 0, own_half(w, 0), placed(w, d, 0), here_x),
+            wcopy(w, 1, own_half(w, 1), placed(w, d, 1), here_y),
+            wcopy(w, 2, own_half(w, 1), placed(w, d, 1), here_x),
+            wcopy(w, 3, own_half(w, 0), placed(w, d, 0), here_y),
+            wcopy(w, 4, placed(w, dx, 0), placed(w, dx, 0), here_y),
+            wcopy(w, 5, placed(w, dy, 1), placed(w, dy, 1), here_x),
+        )
+
+    def block(a, owner):
+        return blocks[a][1].at[owner]
+
+    def zcopy(a, way, s):
+        step = 1 if way == 0 else -1
+        owner = (z - step * s) * 2 + core
+        src = blocks[a][0] if s == 0 else block(a, owner)
+        return pltpu.make_async_remote_copy(
+            src_ref=src, dst_ref=block(a, owner), send_sem=zsend.at[a, way, s],
+            recv_sem=zrecv.at[a, way, s], device_id=(d, e + 2 * step), device_id_type=MESH,
+        )
+
+    def zhas(way, s):
+        if way == 0:
+            return jnp.logical_and(z < chips - 1, z >= s)
+        return jnp.logical_and(z > 0, z + s < chips)
+
+    def zgets(way, s):
+        return z - 1 - s >= 0 if way == 0 else z + 1 + s < chips
+
+    def ccopy(a, way, s):
+        step = 1 if way == 0 else -1
+        owner = e if s < 0 else (z - step * (s + 1)) * 2 + core
+        src = blocks[a][0] if s < 0 else block(a, owner)
+        k = 0 if s < 0 else 1 + way * (chips - 1) + s
+        return pltpu.make_async_remote_copy(
+            src_ref=src, dst_ref=block(a, owner), send_sem=csend.at[a, k],
+            recv_sem=crecv.at[a, k], device_id=(d, sibling), device_id_type=MESH,
+        )
+
+    order = (2, 0, 1)
+    for a in order:
+        for way in (0, 1):
+            @pl.when(zhas(way, 0))
+            def _(a=a, way=way):
+                zcopy(a, way, 0).start()
+    sent = [wcopies(w) for w in range(3)]
+    for w in range(3):
+        for k in range(4):
+            sent[w][k].start()
+    for a in order:
+        ccopy(a, 0, -1).start()
+    here = [
+        pltpu.make_async_copy(weights[w][0].at[0], weights[w][1].at[pl.ds(pl.multiple_of(d * rows, rows), rows), :], local.at[w])
+        for w in range(3)
+    ] + [pltpu.make_async_copy(blocks[a][0], block(a, e), local.at[3 + a]) for a in range(3)]
+    for c in here:
+        c.start()
+
+    def zstep(a, s):
+        for way in (0, 1):
+            @pl.when(zgets(way, s))
+            def _(way=way):
+                zcopy(a, way, s).wait_recv()
+                if s < chips - 2:
+                    @pl.when(zhas(way, s + 1))
+                    def _():
+                        zcopy(a, way, s + 1).start()
+                ccopy(a, way, s).start()
+
+    def wstep(w):
+        sent[w][0].wait_recv()
+        sent[w][4].start()
+        sent[w][1].wait_recv()
+        sent[w][5].start()
+
+    steps = [(s, a) for s in range(chips - 1) for a in order]
+    at = 0
+    for i, (s, a) in enumerate(steps):
+        zstep(a, s)
+        if a != 2 and at < 3:
+            wstep(at)
+            at += 1
+    while at < 3:
+        wstep(at)
+        at += 1
+    for c in here:
+        c.wait()
+    for w in range(3):
+        for k in range(2, 6):
+            sent[w][k].wait_recv()
+        for k in range(6):
+            sent[w][k].wait_send()
+    for a in order:
+        for s in range(-1, chips - 1):
+            for way in (0, 1):
+                if s < 0:
+                    if way == 0:
+                        ccopy(a, 0, -1).wait()
+                    continue
+
+                @pl.when(zhas(way, s))
+                def _(way=way, s=s):
+                    zcopy(a, way, s).wait_send()
+
+                @pl.when(zgets(way, s))
+                def _(way=way, s=s):
+                    ccopy(a, way, s).wait()
+
+
+def scatter_kernel(
+    members,
+    pg, pu, pd, res, gin,
+    xg, xu, xd, yg, yu, yd, rres, rgin,
+    land, part, wsend, wrecv, asend, arecv, local,
+):
+    d, e, dx, dy, dd = places()
+    rows = xg.shape[0]
+    half = rows // 2
+    here_x, here_y = (dx, e), (dy, e)
+
+    barrier = pltpu.get_barrier_semaphore()
+    pl.semaphore_signal(barrier, inc=1, device_id=here_x, device_id_type=MESH)
+    pl.semaphore_signal(barrier, inc=1, device_id=here_y, device_id_type=MESH)
+    for k in range(1, members):
+        pl.semaphore_signal(
+            barrier, inc=1, device_id=(d, lax.rem(e + k, members)), device_id_type=MESH
+        )
+    pl.semaphore_wait(barrier, 1 + members)
+
+    partials = (pg, pu, pd)
+    from_x = (xg, xu, xd)
+    from_y = (yg, yu, yd)
+
+    def piece(w, owner, h):
+        return partials[w].at[pl.ds(pl.multiple_of(owner * rows + h * half, half), half), :]
+
+    def wcopy(w, kind, src, dst, device):
+        return pltpu.make_async_remote_copy(
+            src_ref=src, dst_ref=dst, send_sem=wsend.at[w, kind], recv_sem=wrecv.at[w, kind],
+            device_id=device, device_id_type=MESH,
+        )
+
+    def spot(ref, h):
+        return ref.at[pl.ds(h * half, half), :]
+
+    def wcopies(w):
+        return (
+            wcopy(w, 0, piece(w, dd, 0), land.at[w, 0], here_x),
+            wcopy(w, 1, piece(w, dd, 1), land.at[w, 1], here_y),
+            wcopy(w, 2, piece(w, dx, 0), spot(from_x[w], 0), here_x),
+            wcopy(w, 3, piece(w, dy, 1), spot(from_y[w], 1), here_y),
+            wcopy(w, 4, part.at[w, 0], spot(from_y[w], 0), here_y),
+            wcopy(w, 5, part.at[w, 1], spot(from_x[w], 1), here_x),
+        )
+
+    sent = [wcopies(w) for w in range(3)]
+    moves = ((res, rres), (gin, rgin))
+    far = []
+    for a in (0, 1):
+        src, dst = moves[a]
+        for k in range(1, members):
+            to = lax.rem(e + k, members)
+            far.append(
+                pltpu.make_async_remote_copy(
+                    src_ref=src.at[to], dst_ref=dst.at[e], send_sem=asend.at[a, k],
+                    recv_sem=arecv.at[a, k], device_id=(d, to), device_id_type=MESH,
+                )
+            )
+    for w in range(3):
+        sent[w][0].start()
+        sent[w][1].start()
+    for c in far:
+        c.start()
+    for w in range(3):
+        sent[w][2].start()
+        sent[w][3].start()
+    here = [
+        pltpu.make_async_copy(moves[a][0].at[e], moves[a][1].at[e], local.at[a]) for a in (0, 1)
+    ]
+    for c in here:
+        c.start()
+    tile = half // 4
+    for w in range(3):
+        for h, owner in ((0, dy), (1, dx)):
+            sent[w][h].wait_recv()
+
+            @pl.loop(0, 4)
+            def _(i, w=w, h=h, owner=owner):
+                at = pl.ds(pl.multiple_of(i * tile, tile), tile)
+                mine = partials[w][
+                    pl.ds(pl.multiple_of(owner * rows + h * half + i * tile, tile), tile), :
+                ]
+                part[w, h, at, :] = (
+                    land[w, h, at, :].astype(jnp.float32) + mine.astype(jnp.float32)
+                ).astype(jnp.bfloat16)
+
+            sent[w][4 + h].start()
+    for c in here:
+        c.wait()
+    for c in far:
+        c.wait()
+    for w in range(3):
+        for k in range(2, 6):
+            sent[w][k].wait_recv()
+        for k in range(6):
+            sent[w][k].wait_send()
+
+
+def square_shards(
+    tokens, expert_ids, gate_level, cost_bucket, gate_table,
+    gate_weight, up_weight, down_weight, out_grad,
+):
+    n_tok, width = tokens.shape
+    top_count = expert_ids.shape[1]
+    members = lax.axis_size("expert")
+    n_dp = lax.axis_size("dp")
+    chips = members // 2
+    cap = min(n_tok, 4 * n_tok * top_count // (3 * members))
+    shard = gate_weight.shape[1]
+    units = gate_weight.shape[2]
+    f32, bf16 = jnp.float32, jnp.bfloat16
+    any_spec = pl.BlockSpec(memory_space=pl.ANY)
+    vmem_spec = pl.BlockSpec(memory_space=pltpu.VMEM)
+
+    bucket_tok = jnp.repeat(cost_bucket, n_tok // cost_bucket.shape[0])
+    bucket_hot = bucket_tok[:, None] == jnp.arange(gate_table.shape[0], dtype=jnp.int32)[None, :]
+    table_rows = jnp.sum(jnp.where(bucket_hot[:, :, None], gate_table[None], 0.0), axis=1)
+    level_hot = (
+        gate_level[:, :, None] == jnp.arange(gate_table.shape[1], dtype=jnp.int32)[None, None, :]
+    )
+    gate_values = jnp.sum(jnp.where(level_hot, table_rows[:, None, :], 0.0), axis=2)
+    chosen = expert_ids[None] == jnp.arange(members, dtype=jnp.int32)[:, None, None]
+    mask = jnp.sum(chosen.astype(f32), axis=2)
+    gates = jnp.sum(jnp.where(chosen, gate_values[None], 0.0), axis=2)
+    meta = jnp.concatenate([gates, mask], axis=0)
+
+    def slots(choice):
+        upto = jnp.arange(n_tok)[:, None] < jnp.arange(n_tok)[None, :]
+        rank = jnp.dot(choice.astype(bf16), upto.astype(bf16), preferred_element_type=f32)
+        same = rank[:, None, :] == jnp.arange(cap, dtype=f32)[None, :, None]
+        return jnp.logical_and(same, choice[:, None, :] > 0.5)
+
+    sds = jax.ShapeDtypeStruct
+    w_gate, w_up, w_down, all_tok, all_grd, all_meta = pl.pallas_call(
+        functools.partial(gather_kernel, chips),
+        out_shape=[sds((n_dp * shard, units), bf16)] * 3
+        + [sds((members, n_tok, width), bf16)] * 2
+        + [sds((members, 2 * members, n_tok), f32)],
+        in_specs=[any_spec] * 6,
+        out_specs=[any_spec] * 6,
+        scratch_shapes=[
+            pltpu.SemaphoreType.DMA((3, 6)),
+            pltpu.SemaphoreType.DMA((3, 6)),
+            pltpu.SemaphoreType.DMA((3, 2, chips - 1)),
+            pltpu.SemaphoreType.DMA((3, 2, chips - 1)),
+            pltpu.SemaphoreType.DMA((3, 2 * chips - 1)),
+            pltpu.SemaphoreType.DMA((3, 2 * chips - 1)),
+            pltpu.SemaphoreType.DMA((6,)),
+        ],
+        compiler_params=pltpu.CompilerParams(collective_id=0, has_side_effects=True),
+    )(gate_weight, up_weight, down_weight, tokens, out_grad, meta)
+
+    me = lax.axis_index("expert")
+    my_gate = lax.dynamic_index_in_dim(all_meta, me, 1, keepdims=False)
+    my_mask = lax.dynamic_index_in_dim(all_meta, members + me, 1, keepdims=False)
+    pick = slots(my_mask)
+    slot_gate = jnp.sum(jnp.where(pick, my_gate[:, None, :], 0.0), axis=2)
+    pick = pick.astype(bf16)
+    batched = (((2,), (1,)), ((0,), (0,)))
+    total = members * cap
+    rows = lax.dot_general(pick, all_tok, batched, preferred_element_type=f32)
+    rows = rows.astype(bf16).reshape(total, width)
+    grad_rows = lax.dot_general(pick, all_grd, batched, preferred_element_type=f32)
+    grad_rows = (grad_rows * slot_gate[:, :, None]).astype(bf16).reshape(total, width)
+
+    contract_last = (((1,), (1,)), ((), ()))
+    contract_first = (((0,), (0,)), ((), ()))
+    gate_act = jnp.dot(rows, w_gate, preferred_element_type=f32)
+    up_act = jnp.dot(rows, w_up, preferred_element_type=f32)
+    grad_hidden = jnp.dot(grad_rows, w_down, preferred_element_type=f32)
+    sig = jax.nn.sigmoid(gate_act)
+    swish = gate_act * sig
+    hidden = (swish * up_act).astype(bf16)
+    grad_gate = (grad_hidden * up_act * sig * (1.0 + gate_act * (1.0 - sig))).astype(bf16)
+    grad_up = (grad_hidden * swish).astype(bf16)
+    result = lax.dot_general(hidden, w_down, contract_last, preferred_element_type=f32)
+    result = result.astype(bf16).reshape(members, cap, width)
+    grad_in = lax.dot_general(
+        grad_gate, w_gate, contract_last, preferred_element_type=f32
+    ) + lax.dot_general(grad_up, w_up, contract_last, preferred_element_type=f32)
+    grad_in = grad_in.astype(bf16).reshape(members, cap, width)
+    partials = [
+        lax.dot_general(a, b, contract_first, preferred_element_type=f32).astype(bf16)
+        for a, b in ((rows, grad_gate), (rows, grad_up), (grad_rows, hidden))
+    ]
+
+    half = shard // 2
+    back = pl.pallas_call(
+        functools.partial(scatter_kernel, members),
+        out_shape=[sds((shard, units), bf16)] * 6 + [sds((members, cap, width), bf16)] * 2,
+        in_specs=[vmem_spec] * 3 + [any_spec] * 2,
+        out_specs=[any_spec] * 8,
+        scratch_shapes=[
+            pltpu.VMEM((3, 2, half, units), bf16),
+            pltpu.VMEM((3, 2, half, units), bf16),
+            pltpu.SemaphoreType.DMA((3, 6)),
+            pltpu.SemaphoreType.DMA((3, 6)),
+            pltpu.SemaphoreType.DMA((2, members)),
+            pltpu.SemaphoreType.DMA((2, members)),
+            pltpu.SemaphoreType.DMA((2,)),
+        ],
+        compiler_params=pltpu.CompilerParams(
+            collective_id=1, has_side_effects=True, vmem_limit_bytes=40 * 1024 * 1024
+        ),
+    )(*partials, result, grad_in)
+
+    own = lax.axis_index("dp") * shard
+    grads = [
+        (
+            lax.dynamic_slice_in_dim(partials[w], own, shard, 0).astype(f32)
+            + back[w].astype(f32)
+            + back[3 + w].astype(f32)
+        )[None]
+        for w in range(3)
+    ]
+    place = slots(mask)
+    weight = jnp.where(place, gates[:, None, :], 0.0).reshape(total, n_tok)
+    high = weight.astype(bf16)
+    low = (weight - high.astype(f32)).astype(bf16)
+    returned = back[6].reshape(total, width)
+    output = lax.dot_general(
+        jnp.concatenate([high, low], axis=1), returned, contract_first, preferred_element_type=f32
+    )
+    output = (output[:n_tok] + output[n_tok:]).astype(bf16)
+    token_grad = lax.dot_general(
+        place.reshape(total, n_tok).astype(bf16),
+        back[7].reshape(total, width),
+        contract_first,
+        preferred_element_type=f32,
+    ).astype(bf16)
+    return (output, token_grad, *grads)
 
 
 def move_rows(buffer):
@@ -40,7 +436,12 @@
     marks_hot = (flat_ids[:, None] == jnp.arange(members, dtype=jnp.int32)[None, :]).astype(
         jnp.int32
     )
-    earlier = jnp.cumsum(marks_hot, axis=0) - marks_hot
+    before = jnp.arange(pair_total)[:, None] > jnp.arange(pair_total)[None, :]
+    earlier = jnp.dot(
+        before.astype(jnp.bfloat16),
+        marks_hot.astype(jnp.bfloat16),
+        preferred_element_type=jnp.float32,
+    ).astype(jnp.int32)
     slot_index = jnp.sum(earlier * marks_hot, axis=1)
     slot_place = flat_ids * capacity + slot_index
     owner_row = (
@@ -124,8 +525,11 @@
 
 
 def solution(mesh):
+    members = mesh.shape["expert"]
+    square = mesh.shape["dp"] == 4 and members % 2 == 0 and 4 <= members <= 16
+
     return jax.shard_map(
-        shards,
+        square_shards if square else shards,
         mesh=mesh,
         in_specs=(
             P(("dp", "expert"), None),

time: 326 us -> 260 us (0.80); the launches traced: 320 us -> 259 us
  Pallas kernels: 0 us -> 207 us
  waiting for transfers between devices: 171 us -> 0 us
  local copies, waits for them, and re-layouts: 44.2 us -> 9.98 us
  starting transfers between devices: 26.9 us -> 0 us
  other arithmetic: 28.3 us -> 12.1 us
  between operations: 14 us -> 0.79 us
  matrix products: 36.1 us -> 29.8 us
    pallas_call x0 -> x2, Pallas kernels: none -> 207 us  [the longest x1 109 us: square_shards(): pl.pallas_call(functools.partial(gather_kernel, chips), out_shape=[sds((n...]
    all_to_all x4 -> x0, waiting for transfers between devices: 157 us -> none  [move_rows(): lax.all_to_all(buffer, 'expert', split_axis=0, concat_axis=0, tiled=True)]
    all_to_all x4 -> x0, starting transfers between devices: 26.8 us -> none  [move_rows(): lax.all_to_all(buffer, 'expert', split_axis=0, concat_axis=0, tiled=True)]
    gather x5 -> x0, local copies, waits for them, and re-layouts: 19.3 us -> none  [the longest x1 6.91 us: shards(): grad_back[slot_place].reshape(local_tokens, top_count, model_width)]
    all_gather x3 -> x0, waiting for transfers between devices: 11.6 us -> none  [the longest x1 11.6 us: shards(): lax.all_gather(gate_weight, 'dp', axis=1, tiled=True)]
    concatenate x2 -> x1, other arithmetic: 11.6 us -> 0.6 us  [square_shards(): meta = jnp.concatenate([gates, mask], axis=0)]
    reduce_sum x4, other arithmetic: 11 us -> 2.31 us  [the longest x1 0.77 us: square_shards(): jnp.sum(jnp.where(bucket_hot[:, :, None], gate_table[None], 0.0), axis=1)]
    broadcast_in_dim x0 -> x2, other arithmetic: none -> 7.18 us  [square_shards(): (lax.dynamic_slice_in_dim(partials[w], own, shard, 0).astype(f32) + back[...]
  transfers between devices with their start and end apart: 8 -> 0, of which waited for: 5 -> 0; matrix products, arithmetic and copies ran while one was open for 23% -> 0% of each run, Pallas kernels for 0% -> 0%
where the time goes in v1:
time: 260 us; the launch traced here: 259 us
  Pallas kernels  207 us (80%)
  matrix products  29.8 us (11%)
  other arithmetic  12.1 us (5%)
  local copies, waits for them, and re-layouts  9.98 us (4%)
    pallas_call x1, Pallas kernels, square_shards(): pl.pallas_call(functools.partial(gather_kernel, chips), out_shape=[sds((n...  109 us
    pallas_call x1, Pallas kernels, square_shards(): pl.pallas_call(functools.partial(scatter_kernel, members), out_shape=[sds...  98 us
    dot_general x3, matrix products, square_shards(): lax.dot_general(a, b, contract_first, preferred_element_type=f32)  10.8 us
    unnamed x23, local copies, waits for them, and re-layouts  7.54 us
    broadcast_in_dim x2, other arithmetic, square_shards(): (lax.dynamic_slice_in_dim(partials[w], own, shard, 0).astype(f32) + back[...  7.18 us

profile of v1, /device:TPU:11, one launch (start us, length us, event | category | flops | bytes accessed | tf_op | source)
XLA Modules:
  0.0 259.3 jit_solution(7332681989400977630)
XLA Ops:
  0.6 0.7 broadcast_in_dim.102
  1.4 0.1 eq.94
  1.5 0.8 select_reduce_fusion.1
  2.2 0.7 select_reduce_fusion.2
  2.9 0.7 select_reduce_fusion.3
  3.6 0.6 pad_maximum_fusion.meta
  4.2 108.7 %shard_map.128 = (bf16[2048,768]{1,0:T(8,128)(2,1)}, bf16[2048,768]{1,0:T(8,128)(2,1)}, bf16[2048,768]{1,0:T(8,128)(2,1)}, bf16[8,128,2048]{2,1,0:T(8,128)(2,1)}...) custom-call(bf16[1,512,768]{2,1,0:T(8,128)(2,1)} %wg.1, bf16[1,512,768]{2,1,0:T(8,128)(2,1)} %wu.1, ...), custom_call_target="tpu_custom_call" | custom-call | tf_op jit(solution)/shard_map/pallas_call | solution.py:303
  112.9 0.8 broadcast_compare_fusion
  113.7 0.8 dynamic-slice_convert_fusion
  114.5 0.1 fusion.22
  114.6 0.8 constant_dynamic-slice_fusion
  115.4 0.1 select_reduce_fusion
  115.6 0.0 copy-start.8
  115.6 3.1 %multiply_convert_fusion = bf16[8,64,2048]{2,1,0:T(8,128)(2,1)S(1)} fusion(bf16[8,128,2048]{2,1,0:T(8,128)(2,1)} %get-tuple-element.21, f32[8,64]{1,0:T(8,128)S(1)} %select_reduce_fusion, f32[8,128]{1,0:T(8,128)S(1)} %fusion.22, pred[8,128]{1,0:T(8,128)(4,1)S(1)} %bitcast.83), kind=kOutput, calls=%fused_computation.1 | convolution fusion | flops 270663680 | bytes 6298624 | tf_op jit(solution)/shard_map/dot_general | solution.py:332
  118.6 0.1 copy-done.8
  118.7 0.0 copy-start.7
  118.7 1.8 fusion.28
  120.5 0.4 copy-done.7
  120.9 0.0 copy-start.10
  120.9 0.7 convolution_convert_fusion.4
  121.6 1.2 copy-done.10
  122.8 1.8 fusion.29
  124.6 0.1 copy-done.9
  124.7 2.3 multiply_convert_fusion.1
  126.9 1.8 fusion.30
  128.8 1.8 add_convert_fusion
  130.6 1.8 convolution_convert_fusion.3
  132.4 3.8 %convolution_convert_fusion.pd = bf16[2048,768]{1,0:T(8,128)(2,1)} fusion(bf16[512,2048]{1,0:T(8,128)(2,1)S(1)} %bitcast.80, bf16[512,768]{1,0:T(8,128)(2,1)S(1)} %get-tuple-element.35), kind=kOutput, calls=%fused_computation.2 | convolution fusion | flops 1612185600 | bytes 6029312 | tf_op jit(solution)/shard_map/dot_general | solution.py:352
  136.2 3.6 %convolution_convert_fusion.1.pu = bf16[2048,768]{1,0:T(8,128)(2,1)} fusion(bf16[512,2048]{1,0:T(8,128)(2,1)S(1)} %bitcast.77, bf16[512,768]{1,0:T(8,128)(2,1)S(1)} %get-tuple-element.37), kind=kOutput, calls=%fused_computation.3 | convolution fusion | flops 1612185600 | bytes 6029312 | tf_op jit(solution)/shard_map/dot_general | solution.py:352
  139.8 3.5 %convolution_convert_fusion.2.pg = bf16[2048,768]{1,0:T(8,128)(2,1)} fusion(bf16[512,2048]{1,0:T(8,128)(2,1)S(1)} %bitcast.78, bf16[512,768]{1,0:T(8,128)(2,1)S(1)} %get-tuple-element.36), kind=kOutput, calls=%fused_computation.4 | convolution fusion | flops 1612185600 | bytes 6029312 | tf_op jit(solution)/shard_map/dot_general | solution.py:352
  143.3 98.0 %shard_map.129 = (bf16[512,768]{1,0:T(8,128)(2,1)S(1)}, bf16[512,768]{1,0:T(8,128)(2,1)S(1)}, bf16[512,768]{1,0:T(8,128)(2,1)S(1)}, bf16[512,768]{1,0:T(8,128)(2...) custom-call(bf16[2048,768]{1,0:T(8,128)(2,1)} %convolution_convert_f, ...), custom_call_target="tpu_custom_call" | custom-call | tf_op jit(solution)/shard_map/pallas_call | solution.py:357
  241.3 0.0 copy-start
  241.3 1.3 copy-done
  242.6 0.9 copy-done.1
  243.5 0.9 copy-done.3
  244.4 0.9 copy-done.4
  245.3 0.9 copy-done.5
  246.2 0.9 copy-done.6
  247.1 4.6 %add_bitcast_fusion = (f32[1,512,768]{2,1,0:T(8,128)}, f32[1,512,768]{2,1,0:T(8,128)}) fusion(bf16[512,768]{1,0:T(8,128)(2,1)} %copy-done.6, bf16[512,768]{1,0:T(8,128)(2,1)} %copy-done.4, bf16[2048,768]{1,0:T(8,128)(2,1)} %convolution_convert_fusion.pd, s32[]{:T(128)S(6)} %select_n.39, bf16[512,768]{1,0:T(8,128)(2,1)} %copy-done.5, ...), kind=kLoop, calls=%fused_computation.9 | loop fusion | flops 3932160 | bytes 7864324 | tf_op jit(solution)/shard_map/broadcast_in_dim | solution.py:378
  251.6 0.0 copy-done.2
  251.6 2.6 %add_bitcast_fusion.2 = f32[1,512,768]{2,1,0:T(8,128)} fusion(bf16[512,768]{1,0:T(8,128)(2,1)S(1)} %copy-done.2, bf16[512,768]{1,0:T(8,128)(2,1)S(1)} %get-tuple-element.27, bf16[2048,768]{1,0:T(8,128)(2,1)} %convolution_convert_fusion.2.pg, s32[]{:T(128)S(6)} %select_n.39), kind=kLoop, calls=%fused_computation.11 | loop fusion | flops 1966080 | bytes 3932164 | tf_op jit(solution)/shard_map/broadcast_in_dim | solution.py:378
  254.3 0.1 fusion.23
  254.4 0.1 eq.88
  254.5 0.1 fusion.8
  254.6 0.1 fusion.9
  254.8 2.3 fusion.3
  257.1 0.9 fusion.2
  258.0 1.3 fusion
  (11 shorter events, 0.0 us)
Async XLA Ops:
  115.6 3.2 %copy-start.8 = (bf16[2048,768]{1,0:T(8,128)(2,1)S(1)}, bf16[2048,768]{1,0:T(8,128)(2,1)}, u32[]{:S(2)}) copy-start(bf16[2048,768]{1,0:T(8,128)(2,1)} %get-tuple-element.22) | copy-start | bytes 9437188
  118.7 2.2 copy-start.7
  120.9 1.9 copy-start.10
  122.8 1.9 copy-start.9
  241.3 1.3 copy-start
  242.6 0.9 copy-start.1
  243.5 0.9 copy-start.3
  244.4 0.9 copy-start.4
  245.3 0.9 copy-start.5
  246.2 0.9 copy-start.6
  247.1 4.6 %copy-start.2 = (bf16[512,768]{1,0:T(8,128)(2,1)S(1)}, bf16[512,768]{1,0:T(8,128)(2,1)}, u32[]{:S(2)}) copy-start(bf16[512,768]{1,0:T(8,128)(2,1)} %copy-done.1) | copy-start | bytes 2359300

commit v2 on v1

--- a/solution.py
+++ b/solution.py
@@ -104,8 +104,10 @@
                 zcopy(a, way, 0).start()
     sent = [wcopies(w) for w in range(3)]
     for w in range(3):
-        for k in range(4):
-            sent[w][k].start()
+        sent[w][0].start()
+        sent[w][1].start()
+    sent[0][2].start()
+    sent[0][3].start()
     for a in order:
         ccopy(a, 0, -1).start()
     here = [
@@ -131,17 +133,16 @@
         sent[w][4].start()
         sent[w][1].wait_recv()
         sent[w][5].start()
-
-    steps = [(s, a) for s in range(chips - 1) for a in order]
-    at = 0
-    for i, (s, a) in enumerate(steps):
-        zstep(a, s)
-        if a != 2 and at < 3:
-            wstep(at)
-            at += 1
-    while at < 3:
-        wstep(at)
-        at += 1
+        if w > 0:
+            sent[w][2].start()
+            sent[w][3].start()
+
+    for i in range(chips - 1):
+        for a in order:
+            zstep(a, i)
+        if i == 0:
+            for w in range(3):
+                wstep(w)
     for c in here:
         c.wait()
     for w in range(3):
@@ -168,9 +169,9 @@
 
 def scatter_kernel(
     members,
-    pg, pu, pd, res, gin,
-    xg, xu, xd, yg, yu, yd, rres, rgin,
-    land, part, wsend, wrecv, asend, arecv, local,
+    rows_ref, grad_ref, gg, gu, hid, res, gin,
+    xg, xu, xd, yg, yu, yd, rres, rgin, mg, mu, md,
+    pieces, land, part, wsend, wrecv, asend, arecv, local,
 ):
     d, e, dx, dy, dd = places()
     rows = xg.shape[0]
@@ -186,12 +187,18 @@
         )
     pl.semaphore_wait(barrier, 1 + members)
 
-    partials = (pg, pu, pd)
+    factors = ((rows_ref, gg), (rows_ref, gu), (grad_ref, hid))
+    mine = (mg, mu, md)
     from_x = (xg, xu, xd)
     from_y = (yg, yu, yd)
 
-    def piece(w, owner, h):
-        return partials[w].at[pl.ds(pl.multiple_of(owner * rows + h * half, half), half), :]
+    def product(w, owner, h):
+        left, right = factors[w]
+        columns = pl.ds(pl.multiple_of(owner * rows + h * half, half), half)
+        return lax.dot_general(
+            left[:, columns], right[...], (((0,), (0,)), ((), ())),
+            preferred_element_type=jnp.float32,
+        ).astype(jnp.bfloat16)
 
     def wcopy(w, kind, src, dst, device):
         return pltpu.make_async_remote_copy(
@@ -204,10 +211,10 @@
 
     def wcopies(w):
         return (
-            wcopy(w, 0, piece(w, dd, 0), land.at[w, 0], here_x),
-            wcopy(w, 1, piece(w, dd, 1), land.at[w, 1], here_y),
-            wcopy(w, 2, piece(w, dx, 0), spot(from_x[w], 0), here_x),
-            wcopy(w, 3, piece(w, dy, 1), spot(from_y[w], 1), here_y),
+            wcopy(w, 0, pieces.at[w, 0, 0], land.at[w, 0], here_x),
+            wcopy(w, 1, pieces.at[w, 0, 1], land.at[w, 1], here_y),
+            wcopy(w, 2, pieces.at[w, 1, 0], spot(from_x[w], 0), here_x),
+            wcopy(w, 3, pieces.at[w, 2, 1], spot(from_y[w], 1), here_y),
             wcopy(w, 4, part.at[w, 0], spot(from_y[w], 0), here_y),
             wcopy(w, 5, part.at[w, 1], spot(from_x[w], 1), here_x),
         )
@@ -225,32 +232,39 @@
                     recv_sem=arecv.at[a, k], device_id=(d, to), device_id_type=MESH,
                 )
             )
-    for w in range(3):
-        sent[w][0].start()
-        sent[w][1].start()
     for c in far:
         c.start()
-    for w in range(3):
-        sent[w][2].start()
-        sent[w][3].start()
     here = [
         pltpu.make_async_copy(moves[a][0].at[e], moves[a][1].at[e], local.at[a]) for a in (0, 1)
     ]
     for c in here:
         c.start()
+    for w in range(3):
+        for h in (0, 1):
+            pieces[w, 0, h] = product(w, dd, h)
+            sent[w][h].start()
+    for w in range(3):
+        pieces[w, 1, 0] = product(w, dx, 0)
+        sent[w][2].start()
+        pieces[w, 2, 1] = product(w, dy, 1)
+        sent[w][3].start()
+    for w in range(3):
+        pieces[w, 2, 0] = product(w, dy, 0)
+        pieces[w, 1, 1] = product(w, dx, 1)
+    for w in range(3):
+        for h in (0, 1):
+            mine[w][pl.ds(h * half, half), :] = product(w, d, h)
     tile = half // 4
     for w in range(3):
-        for h, owner in ((0, dy), (1, dx)):
+        for h, slot in ((0, 2), (1, 1)):
             sent[w][h].wait_recv()
 
             @pl.loop(0, 4)
-            def _(i, w=w, h=h, owner=owner):
+            def _(i, w=w, h=h, slot=slot):
                 at = pl.ds(pl.multiple_of(i * tile, tile), tile)
-                mine = partials[w][
-                    pl.ds(pl.multiple_of(owner * rows + h * half + i * tile, tile), tile), :
-                ]
                 part[w, h, at, :] = (
-                    land[w, h, at, :].astype(jnp.float32) + mine.astype(jnp.float32)
+                    land[w, h, at, :].astype(jnp.float32)
+                    + pieces[w, slot, h, at, :].astype(jnp.float32)
                 ).astype(jnp.bfloat16)
 
             sent[w][4 + h].start()
@@ -348,18 +362,15 @@
         grad_gate, w_gate, contract_last, preferred_element_type=f32
     ) + lax.dot_general(grad_up, w_up, contract_last, preferred_element_type=f32)
     grad_in = grad_in.astype(bf16).reshape(members, cap, width)
-    partials = [
-        lax.dot_general(a, b, contract_first, preferred_element_type=f32).astype(bf16)
-        for a, b in ((rows, grad_gate), (rows, grad_up), (grad_rows, hidden))
-    ]
-
     half = shard // 2
     back = pl.pallas_call(
         functools.partial(scatter_kernel, members),
-        out_shape=[sds((shard, units), bf16)] * 6 + [sds((members, cap, width), bf16)] * 2,
-        in_specs=[vmem_spec] * 3 + [any_spec] * 2,
-        out_specs=[any_spec] * 8,
+        out_shape=[sds((shard, units), bf16)] * 6 + [sds((members, cap, width), bf16)] * 2
+        + [sds((shard, units), bf16)] * 3,
+        in_specs=[vmem_spec] * 5 + [any_spec] * 2,
+        out_specs=[any_spec] * 8 + [vmem_spec] * 3,
         scratch_shapes=[
+            pltpu.VMEM((3, 3, 2, half, units), bf16),
             pltpu.VMEM((3, 2, half, units), bf16),
             pltpu.VMEM((3, 2, half, units), bf16),
             pltpu.SemaphoreType.DMA((3, 6)),
@@ -371,12 +382,11 @@
         compiler_params=pltpu.CompilerParams(
             collective_id=1, has_side_effects=True, vmem_limit_bytes=40 * 1024 * 1024
         ),
-    )(*partials, result, grad_in)
-
-    own = lax.axis_index("dp") * shard
+    )(rows, grad_rows, grad_gate, grad_up, hidden, result, grad_in)
+
     grads = [
         (
-            lax.dynamic_slice_in_dim(partials[w], own, shard, 0).astype(f32)
+            back[8 + w].astype(f32)
             + back[w].astype(f32)
             + back[3 + w].astype(f32)
         )[None]

time: 260 us -> 242 us (0.931)
  matrix products: 29.8 us -> 21.6 us
  local copies, waits for them, and re-layouts: 9.98 us -> 5.4 us
  other arithmetic: 12.1 us -> 8.63 us
    dot_general x3 -> x0, matrix products: 10.8 us -> none  [square_shards(): lax.dot_general(a, b, contract_first, preferred_element_type=f32)]
    unnamed x23 -> x15, local copies, waits for them, and re-layouts: 7.54 us -> 2.97 us
    broadcast_in_dim x2, other arithmetic: 7.18 us -> 3.74 us  [square_shards(): (back[8 + w].astype(f32) + back[w].astype(f32) + back[3 + w].astype(f32))...]
where the time goes in v2:
time: 242 us
  Pallas kernels  205 us (85%)
  matrix products  21.6 us (9%)
  other arithmetic  8.63 us (4%)
  local copies, waits for them, and re-layouts  5.4 us (2%)
    pallas_call x1, Pallas kernels, square_shards(): pl.pallas_call(functools.partial(gather_kernel, chips), out_shape=[sds((n...  109 us
    pallas_call x1, Pallas kernels, square_shards(): pl.pallas_call(functools.partial(scatter_kernel, members), out_shape=[sds...  96.7 us

profile of v2, /device:TPU:11, one launch (start us, length us, event | category | flops | bytes accessed | tf_op | source)
XLA Modules:
  0.0 241.7 jit_solution(15632883397349886972)
XLA Ops:
  0.6 0.7 broadcast_in_dim.102
  1.4 0.1 eq.94
  1.5 0.8 select_reduce_fusion.1
  2.2 0.7 select_reduce_fusion.2
  2.9 0.7 select_reduce_fusion.3
  3.6 0.6 pad_maximum_fusion.meta
  4.2 108.7 %shard_map.128 = (bf16[2048,768]{1,0:T(8,128)(2,1)}, bf16[2048,768]{1,0:T(8,128)(2,1)}, bf16[2048,768]{1,0:T(8,128)(2,1)}, bf16[8,128,2048]{2,1,0:T(8,128)(2,1)}...) custom-call(bf16[1,512,768]{2,1,0:T(8,128)(2,1)} %wg.1, bf16[1,512,768]{2,1,0:T(8,128)(2,1)} %wu.1, ...), custom_call_target="tpu_custom_call" | custom-call | tf_op jit(solution)/shard_map/pallas_call | solution.py:317
  112.9 0.8 broadcast_compare_fusion
  113.7 0.8 dynamic-slice_convert_fusion
  114.5 0.1 fusion.22
  114.6 0.8 constant_dynamic-slice_fusion
  115.4 0.1 select_reduce_fusion
  115.5 0.0 copy-start.4
  115.5 3.1 %multiply_convert_fusion = bf16[8,64,2048]{2,1,0:T(8,128)(2,1)S(1)} fusion(bf16[8,128,2048]{2,1,0:T(8,128)(2,1)} %get-tuple-element.24, f32[8,64]{1,0:T(8,128)S(1)} %select_reduce_fusion, f32[8,128]{1,0:T(8,128)S(1)} %fusion.22, pred[8,128]{1,0:T(8,128)(4,1)S(1)} %bitcast.76), kind=kOutput, calls=%fused_computation.1 | convolution fusion | flops 270663680 | bytes 6298624 | tf_op jit(solution)/shard_map/dot_general | solution.py:346
  118.6 0.0 copy-start.2
  118.6 0.1 copy-done.4
  118.7 0.0 copy-start.3
  118.7 1.8 fusion.28
  120.5 0.0 copy-done.2
  120.5 1.1 copy-done.3
  121.6 0.0 copy-start.6
  121.6 0.7 convolution_convert_fusion.1
  122.3 0.0 copy-start.1
  122.3 1.7 copy-done.6
  124.0 0.0 copy-start.5
  124.0 1.8 fusion.29
  125.8 0.0 copy-done.1
  125.8 0.1 copy-done.5
  125.9 2.2 multiply_convert_fusion.1
  128.1 1.8 fusion.30
  130.0 3.1 %add_convert_fusion = bf16[512,2048]{1,0:T(8,128)(2,1)} fusion(f32[512,2048]{1,0:T(8,128)S(1)} %fusion.30, bf16[512,768]{1,0:T(8,128)(2,1)S(1)} %get-tuple-element.43.gu, bf16[2048,768]{1,0:T(8,128)(2,1)S(1)} %copy-done.5), kind=kOutput, calls=%fused_computation | convolution fusion | flops 1612709888 | bytes 10223616 | tf_op jit(solution)/shard_map/dot_general | solution.py:363
  133.1 3.2 %convolution_convert_fusion = bf16[512,2048]{1,0:T(8,128)(2,1)} fusion(bf16[512,768]{1,0:T(8,128)(2,1)S(1)} %get-tuple-element.41.hid, bf16[2048,768]{1,0:T(8,128)(2,1)S(1)} %copy-done.4), kind=kOutput, calls=%fused_computation.2 | convolution fusion | flops 1611661312 | bytes 6029312 | tf_op jit(solution)/shard_map/dot_general | solution.py:359
  136.3 96.7 %shard_map.129 = (bf16[512,768]{1,0:T(8,128)(2,1)S(1)}, bf16[512,768]{1,0:T(8,128)(2,1)S(1)}, bf16[512,768]{1,0:T(8,128)(2,1)S(1)}, bf16[512,768]{1,0:T(8,128)(2...) custom-call(bf16[512,2048]{1,0:T(8,128)(2,1)} %bitcast.69, ...), custom_call_target="tpu_custom_call" | custom-call | tf_op jit(solution)/shard_map/pallas_call | solution.py:366
  232.9 0.0 copy-start
  232.9 2.3 add_bitcast_fusion
  235.3 0.0 copy-done
  235.3 1.4 add_bitcast_fusion.2
  236.7 0.1 fusion.23
  236.8 0.1 eq.88
  236.9 0.1 fusion.8
  237.1 0.1 fusion.9
  237.2 2.3 fusion.3
  239.5 0.9 fusion.2
  240.4 1.3 fusion
  (4 shorter events, 0.0 us)
Async XLA Ops:
  115.5 3.2 %copy-start.4 = (bf16[2048,768]{1,0:T(8,128)(2,1)S(1)}, bf16[2048,768]{1,0:T(8,128)(2,1)}, u32[]{:S(2)}) copy-start(bf16[2048,768]{1,0:T(8,128)(2,1)} %get-tuple-element.25) | copy-start | bytes 9437188
  118.6 1.9 copy-start.2
  118.7 2.9 %copy-start.3 = (bf16[8,128,2048]{2,1,0:T(8,128)(2,1)S(1)}, bf16[8,128,2048]{2,1,0:T(8,128)(2,1)}, u32[]{:S(2)}) copy-start(bf16[8,128,2048]{2,1,0:T(8,128)(2,1)} %get-tuple-element.23) | copy-start | bytes 12582916
  121.6 2.4 %copy-start.6 = (bf16[2048,768]{1,0:T(8,128)(2,1)S(1)}, bf16[2048,768]{1,0:T(8,128)(2,1)}, u32[]{:S(2)}) copy-start(bf16[2048,768]{1,0:T(8,128)(2,1)} %get-tuple-element.27) | copy-start | bytes 9437188
  122.3 3.5 %copy-start.1 = (bf16[8,64,2048]{2,1,0:T(8,128)(2,1)}, bf16[8,64,2048]{2,1,0:T(8,128)(2,1)S(1)}, u32[]{:S(2)}) copy-start(bf16[8,64,2048]{2,1,0:T(8,128)(2,1)S(1)} %convolution_convert_fusion.1) | copy-start | bytes 6291460
  124.0 1.9 copy-start.5
  232.9 2.4 copy-start
